TPU v7x, 32 devices: a whole 2x2x4 slice. The times are simulated.
32 devices in a mesh: dp: 8 (over z, y), tensor: 4 (over x, core).
Axes of the slice: x: 2, y: 2, z: 4, core: 2. Of those that a mesh axis runs over, the one named last changes fastest.
Arguments:
- tokens: bfloat16 [16384, 768], P(('dp', 'tensor')), may hold values from -6 to 6
- query_weight: bfloat16 [768, 768], P('dp', 'tensor'), may hold values from -0.21875 to 0.21875
- w_key: bfloat16 [768, 768], P('dp', 'tensor'), may hold values from -0.21875 to 0.21875
- value_weight: bfloat16 [768, 768], P('dp', 'tensor'), may hold values from -0.21875 to 0.21875
- w_out: bfloat16 [768, 768], P('tensor', 'dp'), may hold values from -0.875 to 0.875
- w_in: bfloat16 [768, 3072], P('dp', 'tensor'), may hold values from -0.21875 to 0.21875
- w_down: bfloat16 [3072, 768], P('tensor', 'dp'), may hold values from -0.109375 to 0.109375
- gain_attn: float32 [768], replicated, may hold values from 0.5 to 1.5
- shift_attn: float32 [768], replicated, may hold values from -0.6 to 0.6
- gain_ffn: float32 [768], replicated, may hold values from 0.5 to 1.5
- shift_ffn: float32 [768], replicated, may hold values from -0.6 to 0.6
- query_down_factor: bfloat16 [768, 8], replicated, may hold values from -0.21875 to 0.21875
- query_up_factor: bfloat16 [8, 768], P(None, 'tensor'), may hold values from -1 to 1
- value_down_factor: bfloat16 [768, 8], replicated, may hold values from -0.21875 to 0.21875
- value_up_factor: bfloat16 [8, 768], P(None, 'tensor'), may hold values from -1 to 1
- lengths: int32 [8, 32], P('dp'), may hold values from 0 to 512, as said below
- cotangent: bfloat16 [16384, 768], P(('dp', 'tensor')), may hold values from -6 to 6
Outputs:
- mixed: bfloat16 [16384, 768], P(('dp', 'tensor'))
- grad_tokens: bfloat16 [16384, 768], P(('dp', 'tensor'))
- grad_a_query: float32 [768, 8], replicated
- query_up_gradient: float32 [8, 768], P(None, 'tensor')
- grad_a_value: float32 [768, 8], replicated
- value_up_gradient: float32 [8, 768], P(None, 'tensor')
Inputs may be any that keep to these rules, and one draw needn't show every extreme that they name: `lengths`: row g lists the sequences of data group g, laid end to end from the group's first position; they cover at most 2048 positions and the rest is padding; 0 marks an empty slot; some group holds a document of 512 tokens.
All inputs are finite; a program needn't handle non-finite values.
Results may differ from a plain program's by a relative error of at most 0.019.
Values may be sent and summed in bfloat16 or wider, within the bound.
A program may use at most 128 MiB of HBM per device.

v0:
```python
import jax
import jax.numpy as jnp
from jax import lax
from jax.sharding import PartitionSpec as P

HEAD_DIM = 64


ADAPTER_SCALE = 2.0
NEG_FILL = -1e30
LN_EPS = 1e-05
HIGH = lax.Precision.HIGHEST


def matrix_product(left, right):
    return jnp.dot(left, right, preferred_element_type=jnp.float32)


def interior_rows(left, right, precision_kind=None):
    return lax.dot_general(
        left,
        right,
        (((0,), (0,)), ((), ())),
        precision=precision_kind,
        preferred_element_type=jnp.float32,
    )


def norm_forward(row_vals, gain_vals, offset):
    middle = jnp.mean(row_vals, axis=-1, keepdims=True)
    centred = row_vals - middle
    inverse = lax.rsqrt(jnp.mean(centred * centred, axis=-1, keepdims=True) + LN_EPS)
    normed = centred * inverse
    return (normed * gain_vals + offset, normed, inverse)


def norm_backward(grad_out, normed, inverse, gain_vals):
    grad_n = grad_out * gain_vals
    return inverse * (
        grad_n
        - jnp.mean(grad_n, axis=-1, keepdims=True)
        - normed * jnp.mean(grad_n * normed, axis=-1, keepdims=True)
    )


def gelu_parts(hidden):
    cdf_part = 0.5 * (1.0 + lax.erf(hidden * 0.7071067811865476))
    density = jnp.exp(-0.5 * hidden * hidden) * 0.3989422804014327
    return (hidden * cdf_part, cdf_part + hidden * density)


def block_scores(q_blk, seg_blk, key_heads, segments, score_scale):
    raw_scores = (
        jnp.einsum("qhe,khe->hqk", q_blk, key_heads, preferred_element_type=jnp.float32)
        * score_scale
    )
    allowed = seg_blk[:, None] == segments[None, :]
    return jnp.where(allowed[None], raw_scores, NEG_FILL)


def attend_forward(query_heads, key_heads, value_heads, segments, score_scale):
    total_rows, heads_here, head_size = query_heads.shape
    block_rows = min(512, total_rows)
    block_count = total_rows // block_rows
    q_blocks = query_heads.reshape(block_count, block_rows, heads_here, head_size)
    seg_blocks = segments.reshape(block_count, block_rows)

    def block_step(running, block_in):
        q_blk, seg_blk = block_in
        scores = block_scores(q_blk, seg_blk, key_heads, segments, score_scale)
        row_top = jnp.max(scores, axis=-1, keepdims=True)
        exp_scores = jnp.exp(scores - row_top)
        row_sum = jnp.sum(exp_scores, axis=-1, keepdims=True)
        softmax_low = (exp_scores / row_sum).astype(jnp.bfloat16)
        block_out = jnp.einsum(
            "hqk,khe->qhe", softmax_low, value_heads, preferred_element_type=jnp.float32
        )
        return (running, (block_out.astype(jnp.bfloat16), row_top + jnp.log(row_sum)))

    unused, (outputs, lse_blocks) = lax.scan(
        block_step, jnp.zeros((), jnp.float32), (q_blocks, seg_blocks)
    )
    return (outputs.reshape(total_rows, heads_here * head_size), lse_blocks)


def attend_backward(
    query_heads, key_heads, value_heads, segments, lse_blocks, grad_heads, score_scale
):
    total_rows, heads_here, head_size = query_heads.shape
    block_rows = min(512, total_rows)
    block_count = total_rows // block_rows
    q_blocks = query_heads.reshape(block_count, block_rows, heads_here, head_size)
    seg_blocks = segments.reshape(block_count, block_rows)
    grad_blocks = grad_heads.reshape(block_count, block_rows, heads_here, head_size)

    def block_step(running, block_in):
        key_acc, value_acc = running
        q_blk, seg_blk, grad_blk, lse_blk = block_in
        scores = block_scores(q_blk, seg_blk, key_heads, segments, score_scale)
        softmax_w = jnp.exp(scores - lse_blk)
        softmax_low = softmax_w.astype(jnp.bfloat16)
        grad_prob = jnp.einsum(
            "qhe,khe->hqk", grad_blk, value_heads, preferred_element_type=jnp.float32
        )
        row_dot = jnp.sum(softmax_w * grad_prob, axis=-1, keepdims=True)
        grad_score = (softmax_w * (grad_prob - row_dot)).astype(jnp.bfloat16)
        grad_q = (
            jnp.einsum("hqk,khe->qhe", grad_score, key_heads, preferred_element_type=jnp.float32)
            * score_scale
        )
        key_acc = (
            key_acc
            + jnp.einsum("hqk,qhe->khe", grad_score, q_blk, preferred_element_type=jnp.float32)
            * score_scale
        )
        value_acc = value_acc + jnp.einsum(
            "hqk,qhe->khe", softmax_low, grad_blk, preferred_element_type=jnp.float32
        )
        return ((key_acc, value_acc), grad_q)

    zero_heads = jnp.zeros((total_rows, heads_here, head_size), jnp.float32)
    (grad_k, grad_v), grad_q = lax.scan(
        block_step, (zero_heads, zero_heads), (q_blocks, seg_blocks, grad_blocks, lse_blocks)
    )
    width = heads_here * head_size
    return (
        grad_q.reshape(total_rows, width),
        grad_k.reshape(total_rows, width),
        grad_v.reshape(total_rows, width),
    )


def local(
    tokens,
    query_weight,
    w_key,
    value_weight,
    w_out,
    w_in,
    w_down,
    gain_attn,
    shift_attn,
    gain_ffn,
    shift_ffn,
    query_down_factor,
    query_up_factor,
    value_down_factor,
    value_up_factor,
    lengths,
    cotangent,
):
    gathered = (
        lax.all_gather(query_weight, "dp", axis=0, tiled=True),
        lax.all_gather(w_key, "dp", axis=0, tiled=True),
        lax.all_gather(value_weight, "dp", axis=0, tiled=True),
        lax.all_gather(w_out, "dp", axis=1, tiled=True),
        lax.all_gather(w_in, "dp", axis=0, tiled=True),
        lax.all_gather(w_down, "dp", axis=1, tiled=True),
    )
    query_complete, full_key, value_complete, full_out, full_in, full_down = gathered
    rows_per_group = lax.all_gather(tokens, "tensor", axis=0, tiled=True)
    total_rows = rows_per_group.shape[0]
    heads_here = query_complete.shape[1] // HEAD_DIM
    score_scale = HEAD_DIM ** (-0.5)
    slot_ends = jnp.cumsum(lengths[0])
    places = jnp.arange(total_rows, dtype=jnp.int32)
    segments = jnp.sum((slot_ends[None, :] <= places[:, None]).astype(jnp.int32), axis=1)
    query_lifted = matrix_product(rows_per_group, query_down_factor).astype(jnp.bfloat16)
    query_rows = (
        matrix_product(rows_per_group, query_complete)
        + ADAPTER_SCALE * matrix_product(query_lifted, query_up_factor)
    ).astype(jnp.bfloat16)
    keys_all = matrix_product(rows_per_group, full_key).astype(jnp.bfloat16)
    value_lifted = matrix_product(rows_per_group, value_down_factor).astype(jnp.bfloat16)
    value_rows_every = (
        matrix_product(rows_per_group, value_complete)
        + ADAPTER_SCALE * matrix_product(value_lifted, value_up_factor)
    ).astype(jnp.bfloat16)
    head_shape = (total_rows, heads_here, HEAD_DIM)
    query_heads = query_rows.reshape(head_shape)
    key_heads = keys_all.reshape(head_shape)
    value_heads = value_rows_every.reshape(head_shape)
    context, lse_blocks = attend_forward(query_heads, key_heads, value_heads, segments, score_scale)
    attn_terms = matrix_product(context, full_out)
    attn_local = lax.psum_scatter(attn_terms, "tensor", scatter_dimension=0, tiled=True)
    first_f, normed_one, inverse_one = norm_forward(
        tokens.astype(jnp.float32) + attn_local, gain_attn, shift_attn
    )
    first_local = first_f.astype(jnp.bfloat16)
    first_all = lax.all_gather(first_local, "tensor", axis=0, tiled=True)
    hidden = matrix_product(first_all, full_in)
    acted_f, slope = gelu_parts(hidden)
    acted = acted_f.astype(jnp.bfloat16)
    ffn_local = lax.psum_scatter(
        matrix_product(acted, full_down).astype(jnp.bfloat16),
        "tensor",
        scatter_dimension=0,
        tiled=True,
    ).astype(jnp.float32)
    mixed_f, normed_two, inverse_two = norm_forward(
        first_local.astype(jnp.float32) + ffn_local, gain_ffn, shift_ffn
    )
    mixed = mixed_f.astype(jnp.bfloat16)
    grad_two = norm_backward(cotangent.astype(jnp.float32), normed_two, inverse_two, gain_ffn)
    grad_ffn_all = lax.all_gather(grad_two.astype(jnp.bfloat16), "tensor", axis=0, tiled=True)
    grad_hidden = (matrix_product(grad_ffn_all, full_down.T) * slope).astype(jnp.bfloat16)
    grad_first = grad_two + lax.psum_scatter(
        matrix_product(grad_hidden, full_in.T).astype(jnp.bfloat16),
        "tensor",
        scatter_dimension=0,
        tiled=True,
    ).astype(jnp.float32)
    grad_one = norm_backward(grad_first, normed_one, inverse_one, gain_attn)
    grad_attn_all = lax.all_gather(grad_one.astype(jnp.bfloat16), "tensor", axis=0, tiled=True)
    grad_context = matrix_product(grad_attn_all, full_out.T).astype(jnp.bfloat16)
    grad_q, grad_k, grad_v = attend_backward(
        query_heads,
        key_heads,
        value_heads,
        segments,
        lse_blocks,
        grad_context.reshape(head_shape),
        score_scale,
    )
    query_narrow_gradient = grad_q.astype(jnp.bfloat16)
    grad_k_low = grad_k.astype(jnp.bfloat16)
    value_narrow_gradient = grad_v.astype(jnp.bfloat16)
    query_lifted_gradient = ADAPTER_SCALE * matrix_product(query_narrow_gradient, query_up_factor.T)
    value_lifted_gradient = ADAPTER_SCALE * matrix_product(value_narrow_gradient, value_up_factor.T)
    query_up_gradient = ADAPTER_SCALE * interior_rows(query_lifted, query_narrow_gradient)
    value_up_gradient = ADAPTER_SCALE * interior_rows(value_lifted, value_narrow_gradient)
    rows_float = rows_per_group.astype(jnp.float32)
    grad_a_query = interior_rows(rows_float, query_lifted_gradient, HIGH)
    grad_a_value = interior_rows(rows_float, value_lifted_gradient, HIGH)
    grad_rows = (
        matrix_product(query_narrow_gradient, query_complete.T)
        + matrix_product(grad_k_low, full_key.T)
        + matrix_product(value_narrow_gradient, value_complete.T)
    )
    grad_rows = grad_rows + jnp.dot(
        query_lifted_gradient, query_down_factor.astype(jnp.float32).T, precision=HIGH
    )
    grad_rows = grad_rows + jnp.dot(
        value_lifted_gradient, value_down_factor.astype(jnp.float32).T, precision=HIGH
    )
    grad_tokens = (
        grad_one
        + lax.psum_scatter(
            grad_rows.astype(jnp.bfloat16), "tensor", scatter_dimension=0, tiled=True
        ).astype(jnp.float32)
    ).astype(jnp.bfloat16)
    b_sums = lax.psum((query_up_gradient, value_up_gradient), "dp")
    a_sums = lax.psum((grad_a_query, grad_a_value), ("dp", "tensor"))
    total_aq, total_av = a_sums
    total_bq, total_bv = b_sums
    return (mixed, grad_tokens, total_aq, total_bq, total_av, total_bv)


def solution(mesh):
    return jax.shard_map(
        local,
        mesh=mesh,
        in_specs=(
            P(("dp", "tensor"), None),
            P("dp", "tensor"),
            P("dp", "tensor"),
            P("dp", "tensor"),
            P("tensor", "dp"),
            P("dp", "tensor"),
            P("tensor", "dp"),
            P(),
            P(),
            P(),
            P(),
            P(),
            P(None, "tensor"),
            P(),
            P(None, "tensor"),
            P("dp", None),
            P(("dp", "tensor"), None),
        ),
        out_specs=(
            P(("dp", "tensor"), None),
            P(("dp", "tensor"), None),
            P(),
            P(None, "tensor"),
            P(),
            P(None, "tensor"),
        ),
        check_vma=False,
    )
```

profile of v0, /device:TPU:0, one launch (start us, length us, event | category | flops | bytes accessed | tf_op | source)
XLA Modules:
  0.0 829.0 jit_solution(8759604822031018100)
XLA Ops:
  11.4 35.3 %all_gather.31 = bf16[768,192]{1,0:T(8,128)(2,1)} all-gather(bf16[96,192]{1,0:T(8,128)(2,1)} %param.22), channel_id=1, replica_groups=mesh['dp'=8,'tensor'=4] {'dp'}, dimensions={0}, use_global_device_ids=true | all-gather | bytes 331776 | tf_op jit(solution)/shard_map/all_gather | solution.py:153
  46.6 33.4 %all_gather.33 = bf16[768,192]{1,0:T(8,128)(2,1)} all-gather(bf16[96,192]{1,0:T(8,128)(2,1)} %param.24), channel_id=1, replica_groups=mesh['dp'=8,'tensor'=4] {'dp'}, dimensions={0}, use_global_device_ids=true | all-gather | bytes 331776 | tf_op jit(solution)/shard_map/all_gather | solution.py:155
  80.0 31.5 %all_gather.32 = bf16[768,192]{1,0:T(8,128)(2,1)S(1)} all-gather(bf16[96,192]{1,0:T(8,128)(2,1)} %param.23), channel_id=1, replica_groups=mesh['dp'=8,'tensor'=4] {'dp'}, dimensions={0}, use_global_device_ids=true | all-gather | bytes 331776 | tf_op jit(solution)/shard_map/all_gather | solution.py:154
  111.5 33.0 %all_gather.34 = bf16[192,768]{0,1:T(8,128)(2,1)} all-gather(bf16[192,96]{0,1:T(8,128)(2,1)S(1)} %copy.43), channel_id=1, replica_groups=mesh['dp'=8,'tensor'=4] {'dp'}, dimensions={1}, use_global_device_ids=true | all-gather | bytes 331776 | tf_op jit(solution)/shard_map/all_gather | solution.py:156
  162.8 97.6 %while.27 = (s32[]{:T(128)}, bf16[4,512,3,64]{1,3,2,0:T(8,128)(2,1)}, f32[4,3,512,1]{2,1,3,0:T(4,128)}, s32[4,512]{1,0:T(4,128)}, s32[2048]{0:T(1024)S(1)}, /*in...) while((s32[]{:T(128)}, ...), condition=%wide.region_5.6_spmd, body=%wide.region_2.5_spmd.sunk | while | flops 844200448 | bytes 47122044 | solution.py:80
  164.2 8.3 fusion.139
  172.5 6.8 fusion.140
  179.9 7.3 fusion.141
  188.6 8.3 fusion.139
  196.9 6.8 fusion.140
  204.3 7.3 fusion.141
  213.0 8.3 fusion.139
  221.3 6.8 fusion.140
  228.7 7.3 fusion.141
  237.4 8.3 fusion.139
  245.7 6.8 fusion.140
  253.1 7.3 fusion.141
  267.2 58.4 %reduce-scatter.5.cloned.1.call-done = f32[512,768]{1,0:T(8,128)} async-done(((f32[2048,768]{1,0:T(8,128)}), f32[512,768]{1,0:T(8,128)}) %reduce-scatter.5.cloned.1.call-update) | async-done | bytes 1572880 | tf_op jit(solution)/shard_map/reduce_scatter | solution.py:185
  329.9 27.8 %all-gather.9.cloned.1.call-done = bf16[2048,768]{1,0:T(8,128)(2,1)} async-done(((bf16[512,768]{1,0:T(8,128)(2,1)}), bf16[2048,768]{1,0:T(8,128)(2,1)}) %all-gather.9.cloned.1.call-update) | async-done | bytes 3145744 | tf_op jit(solution)/shard_map/all_gather | solution.py:190
  357.7 7.5 fusion.61
  365.2 36.4 %all-gather.13.cloned.1.call-done = bf16[768,768]{0,1:T(8,128)(2,1)} async-done(((bf16[768,96]{0,1:T(8,128)(2,1)}), bf16[768,768]{0,1:T(8,128)(2,1)}) %all-gather.13.cloned.1.call-update) | async-done | bytes 1179664 | tf_op jit(solution)/shard_map/all_gather | solution.py:158
  401.6 6.7 convolution_convert_fusion.1
  408.3 36.3 %reduce-scatter.7.cloned.1.call-done = bf16[512,768]{1,0:T(8,128)(2,1)} async-done(((bf16[2048,768]{1,0:T(8,128)(2,1)}), bf16[512,768]{1,0:T(8,128)(2,1)}) %reduce-scatter.7.cloned.1.call-update) | async-done | bytes 786448 | tf_op jit(solution)/shard_map/reduce_scatter | solution.py:194
  451.1 28.4 %all-gather.15.cloned.1.call-done = bf16[2048,768]{1,0:T(8,128)(2,1)} async-done(((bf16[512,768]{1,0:T(8,128)(2,1)}), bf16[2048,768]{1,0:T(8,128)(2,1)}) %all-gather.15.cloned.1.call-update) | async-done | bytes 3145744 | tf_op jit(solution)/shard_map/all_gather | solution.py:205
  479.5 10.2 %convolution_convert_fusion = bf16[2048,768]{1,0:T(8,128)(2,1)} fusion(bf16[768,768]{1,0:T(8,128)(2,1)} %all-gather.11.cloned.1.call-done, f32[2048,768]{1,0:T(8,128)} %fusion.61, bf16[2048,768]{1,0:T(8,128)(2,1)} %all-gather.15.cloned.1.call-done, bf16[768,768]{0,1:T(8,128)(2,1)} %all-gather.13.cloned.1.call-done), kind=kOutput, calls=%fused_computation.61 | convolution fusion | flops 4849139712 | bytes 14942208 | tf_op jit(solution)/shard_map/dot_general | solution.py:16
  489.8 38.1 %reduce-scatter.9.cloned.1.call-done = bf16[512,768]{1,0:T(8,128)(2,1)} async-done(((bf16[2048,768]{1,0:T(8,128)(2,1)}), bf16[512,768]{1,0:T(8,128)(2,1)}) %reduce-scatter.9.cloned.1.call-update) | async-done | bytes 786448 | tf_op jit(solution)/shard_map/reduce_scatter | solution.py:207
  533.3 28.4 %all-gather.17.cloned.1.call-done = bf16[2048,768]{1,0:T(8,128)(2,1)} async-done(((bf16[512,768]{1,0:T(8,128)(2,1)}), bf16[2048,768]{1,0:T(8,128)(2,1)}) %all-gather.17.cloned.1.call-update) | async-done | bytes 3145744 | tf_op jit(solution)/shard_map/all_gather | solution.py:214
  566.4 152.3 %while.28 = (s32[]{:T(128)}, f32[2048,3,64]{0,2,1:T(8,128)}, f32[2048,3,64]{0,2,1:T(8,128)}, bf16[4,512,3,64]{1,3,2,0:T(8,128)(2,1)}, bf16[4,512,3,64]{1,3,2,0:T...) while((s32[]{:T(128)}, f32[2048,3,64]{0,2,1:T(8,128)}, ...), condition=%wide.region_19.20_spmd.clone, body=%wide.region_17.19_spmd.clone.sunk | while | flops 2063563264 | bytes 229043040 | solution.py:122
  573.1 7.0 multiply_reduce_fusion.6
  580.0 6.3 multiply_convert_fusion.4
  586.4 5.5 fusion.152
  591.8 6.2 fusion.154
  598.1 4.9 fusion.153
  610.7 7.0 multiply_reduce_fusion.6
  617.7 6.3 multiply_convert_fusion.4
  624.0 5.9 fusion.152
  629.9 6.2 fusion.154
  648.8 7.0 multiply_reduce_fusion.6
  655.8 6.3 multiply_convert_fusion.4
  662.1 5.9 fusion.152
  668.0 6.2 fusion.154
  686.9 7.0 multiply_reduce_fusion.6
  693.8 6.3 multiply_convert_fusion.4
  700.2 5.9 fusion.152
  706.1 6.2 fusion.154
  730.0 7.7 add_convert_fusion
  740.8 37.7 %all-reduce.1 = (f32[8,192]{1,0:T(8,128)}, f32[8,192]{1,0:T(8,128)}) all-reduce(f32[8,192]{1,0:T(8,128)S(1)} %convolution_multiply_fusion.7, f32[8,192]{1,0:T(8,128)S(1)} %convolution_multiply_fusion.6), channel_id=1, replica_groups=mesh['dp'=8,'tensor'=4] {'dp'}, use_global_device_ids=true, to_apply=%region_22.23 | all-reduce | flops 3072 | bytes 24576 | tf_op jit(solution)/shard_map/psum | solution.py:252
  781.1 37.9 %all-reduce = (f32[768,8]{0,1:T(8,128)}, f32[768,8]{0,1:T(8,128)}) all-reduce(f32[768,8]{0,1:T(8,128)S(1)} %convolution_bitcast_fusion.1, f32[768,8]{0,1:T(8,128)S(1)} %convolution_bitcast_fusion), channel_id=1, replica_groups=mesh['dp'=8,'tensor'=4] {'dp','tensor'}, use_global_device_ids=true, to_apply=%region_21.22 | all-reduce | flops 12288 | bytes 98304 | tf_op jit(solution)/shard_map/psum | solution.py:253
  (245 shorter events, 121.8 us)
Async XLA Ops:
  8.0 136.5 %copy-start = (bf16[768,8]{0,1:T(8,128)(2,1)S(1)}, bf16[768,8]{0,1:T(8,128)(2,1)}, u32[]{:S(2)}) copy-start(bf16[768,8]{0,1:T(8,128)(2,1)} %param.32) | copy-start | bytes 36868
  8.0 136.5 %all-gather.7.cloned.1.call-start = ((), (), s32[]{:S(2)}) async-start(), calls=%async_computation.4 | async-start | bytes 3932160 | tf_op jit(solution)/shard_map/all_gather | solution.py:161
  8.7 316.9 %reduce-scatter.5.cloned.1.call-start = ((), (), s32[]{:S(2)}) async-start(), calls=%async_computation.5 | async-start | bytes 7864320 | tf_op jit(solution)/shard_map/reduce_scatter | solution.py:185
  9.8 134.6 %copy-start.29 = (s32[2048]{0:T(1024)}, s32[2048]{0:T(1024)S(1)}, u32[]{:S(2)}) copy-start(s32[2048]{0:T(1024)S(1)} %convert_reduce_fusion) | copy-start | bytes 24580
  80.0 68.1 %copy-start.39 = (bf16[8,192]{1,0:T(8,128)(2,1)S(1)}, bf16[8,192]{1,0:T(8,128)(2,1)}, u32[]{:S(2)}) copy-start(bf16[8,192]{1,0:T(8,128)(2,1)} %param.33) | copy-start | bytes 9220
  111.5 47.0 %copy-start.17 = (bf16[768,192]{1,0:T(8,128)(2,1)}, bf16[768,192]{1,0:T(8,128)(2,1)S(1)}, u32[]{:S(2)}) copy-start(bf16[768,192]{1,0:T(8,128)(2,1)S(1)} %all_gather.32) | copy-start | bytes 884740
  172.5 7.4 copy-start.9
  196.9 7.4 copy-start.9
  221.3 7.4 copy-start.9
  245.7 7.4 copy-start.9
  266.2 59.5 %copy-start.12 = (bf16[512,768]{1,0:T(8,128)(2,1)S(1)}, bf16[512,768]{1,0:T(8,128)(2,1)}, u32[]{:S(2)}) copy-start(bf16[512,768]{1,0:T(8,128)(2,1)} %param.21) | copy-start | bytes 2359300
  266.2 61.7 %copy-start.37 = (f32[768]{0:T(1024)S(1)}, f32[768]{0:T(1024)}, u32[]{:S(2)}) copy-start(f32[768]{0:T(1024)} %param.28) | copy-start | bytes 9220
  266.2 61.7 %copy-start.44 = (f32[768]{0:T(1024)S(1)}, f32[768]{0:T(1024)}, u32[]{:S(2)}) copy-start(f32[768]{0:T(1024)} %param.29) | copy-start | bytes 9220
  266.2 63.7 %all-gather.11.cloned.1.call-start = ((), (), s32[]{:S(2)}) async-start(), calls=%async_computation.7 | async-start | bytes 1327104 | tf_op jit(solution)/shard_map/all_gather | solution.py:157
  266.8 90.9 %all-gather.9.cloned.1.call-start = ((), (), s32[]{:S(2)}) async-start(), calls=%async_computation.6 | async-start | bytes 3932160 | tf_op jit(solution)/shard_map/all_gather | solution.py:190
  327.9 37.3 %copy-start.38 = (f32[512]{0:T(512)}, f32[512]{0:T(512)S(1)}, u32[]{:S(2)}) copy-start(f32[512]{0:T(512)S(1)} %add_rsqrt_fusion.1) | copy-start | bytes 6148
  329.2 72.3 %all-gather.13.cloned.1.call-start = ((), (), s32[]{:S(2)}) async-start(), calls=%async_computation.8 | async-start | bytes 1327104 | tf_op jit(solution)/shard_map/all_gather | solution.py:158
  329.8 114.9 %reduce-scatter.7.cloned.1.call-start = ((), (), s32[]{:S(2)}) async-start(), calls=%async_computation.9 | async-start | bytes 3932160 | tf_op jit(solution)/shard_map/reduce_scatter | solution.py:194
  408.3 36.4 %copy-start.11 = (bf16[512,768]{1,0:T(8,128)(2,1)S(1)}, bf16[512,768]{1,0:T(8,128)(2,1)}, u32[]{:S(2)}) copy-start(bf16[512,768]{1,0:T(8,128)(2,1)} %add_convert_fusion.3) | copy-start | bytes 2359300
  408.3 71.2 %all-gather.15.cloned.1.call-start = ((), (), s32[]{:S(2)}) async-start(), calls=%async_computation.10 | async-start | bytes 3932160 | tf_op jit(solution)/shard_map/all_gather | solution.py:205
  451.0 76.8 %reduce-scatter.9.cloned.1.call-start = ((), (), s32[]{:S(2)}) async-start(), calls=%async_computation.11 | async-start | bytes 3932160 | tf_op jit(solution)/shard_map/reduce_scatter | solution.py:207
  489.7 71.9 %all-gather.17.cloned.1.call-start = ((), (), s32[]{:S(2)}) async-start(), calls=%async_computation.12 | async-start | bytes 3932160 | tf_op jit(solution)/shard_map/all_gather | solution.py:214
  533.2 285.8 %reduce-scatter.11.cloned.1.call-start = ((), (), s32[]{:S(2)}) async-start(), calls=%async_computation.13 | async-start | bytes 3932160 | tf_op jit(solution)/shard_map/reduce_scatter | solution.py:248
  533.3 33.1 %copy-start.6 = (bf16[2048,3,64]{0,2,1:T(8,128)(2,1)S(1)}, bf16[2048,3,64]{0,2,1:T(8,128)(2,1)}, u32[]{:S(2)}) copy-start(bf16[2048,3,64]{0,2,1:T(8,128)(2,1)} %get-tuple-element.483) | copy-start | bytes 2359300
  533.3 33.1 %copy-start.31 = (s32[2048]{0:T(1024)S(1)}, s32[2048]{0:T(1024)}, u32[]{:S(2)}) copy-start(s32[2048]{0:T(1024)} %copy-done.29) | copy-start | bytes 24580
  569.3 10.7 %copy-start.1 = (f32[3,512,2048]{2,1,0:T(8,128)}, f32[3,512,2048]{2,1,0:T(8,128)S(1)}, u32[]{:S(2)}) copy-start(f32[3,512,2048]{2,1,0:T(8,128)S(1)} %fusion.151) | copy-start | bytes 37748740 | tf_op jit(solution)/shard_map/while
  586.4 11.7 %copy-start.2 = (f32[3,512,2048]{2,1,0:T(8,128)S(1)}, f32[3,512,2048]{2,1,0:T(8,128)}, u32[]{:S(2)}) copy-start(f32[3,512,2048]{2,1,0:T(8,128)} %copy-done.1) | copy-start | bytes 37748740 | tf_op jit(solution)/shard_map/while
  591.8 6.2 copy-start.3
  591.8 6.2 copy-start.26
  598.1 6.1 copy-start.7
  606.9 10.7 %copy-start.1 = (f32[3,512,2048]{2,1,0:T(8,128)}, f32[3,512,2048]{2,1,0:T(8,128)S(1)}, u32[]{:S(2)}) copy-start(f32[3,512,2048]{2,1,0:T(8,128)S(1)} %fusion.151) | copy-start | bytes 37748740 | tf_op jit(solution)/shard_map/while
  624.0 12.1 %copy-start.2 = (f32[3,512,2048]{2,1,0:T(8,128)S(1)}, f32[3,512,2048]{2,1,0:T(8,128)}, u32[]{:S(2)}) copy-start(f32[3,512,2048]{2,1,0:T(8,128)} %copy-done.1) | copy-start | bytes 37748740 | tf_op jit(solution)/shard_map/while
  629.9 6.2 copy-start.3
  629.9 6.2 copy-start.26
  636.2 6.1 copy-start.7
  645.0 10.7 %copy-start.1 = (f32[3,512,2048]{2,1,0:T(8,128)}, f32[3,512,2048]{2,1,0:T(8,128)S(1)}, u32[]{:S(2)}) copy-start(f32[3,512,2048]{2,1,0:T(8,128)S(1)} %fusion.151) | copy-start | bytes 37748740 | tf_op jit(solution)/shard_map/while
  662.1 12.2 %copy-start.2 = (f32[3,512,2048]{2,1,0:T(8,128)S(1)}, f32[3,512,2048]{2,1,0:T(8,128)}, u32[]{:S(2)}) copy-start(f32[3,512,2048]{2,1,0:T(8,128)} %copy-done.1) | copy-start | bytes 37748740 | tf_op jit(solution)/shard_map/while
  668.0 6.2 copy-start.3
  668.0 6.2 copy-start.26
  674.2 6.1 copy-start.7
  683.1 10.7 %copy-start.1 = (f32[3,512,2048]{2,1,0:T(8,128)}, f32[3,512,2048]{2,1,0:T(8,128)S(1)}, u32[]{:S(2)}) copy-start(f32[3,512,2048]{2,1,0:T(8,128)S(1)} %fusion.151) | copy-start | bytes 37748740 | tf_op jit(solution)/shard_map/while
  700.2 12.2 %copy-start.2 = (f32[3,512,2048]{2,1,0:T(8,128)S(1)}, f32[3,512,2048]{2,1,0:T(8,128)}, u32[]{:S(2)}) copy-start(f32[3,512,2048]{2,1,0:T(8,128)} %copy-done.1) | copy-start | bytes 37748740 | tf_op jit(solution)/shard_map/while
  706.1 6.3 copy-start.3
  706.1 6.3 copy-start.26
  712.3 6.1 copy-start.7
  724.1 4.7 copy-start.18
  730.0 7.8 copy-start.33
  737.7 40.8 %copy-start.5 = (bf16[2048,768]{1,0:T(8,128)(2,1)S(1)}, bf16[2048,768]{1,0:T(8,128)(2,1)}, u32[]{:S(2)}) copy-start(bf16[2048,768]{1,0:T(8,128)(2,1)} %all-gather.7.cloned.1.call-done) | copy-start | bytes 9437188
  (29 other events, 61.9 us)
Sparse Core Ops, SparseCore 0:
  10.4 31.2 all-gather.6
  266.3 59.2 reduce-scatter.4
  489.9 37.9 reduce-scatter.8
  737.9 37.9 reduce-scatter.10
Sparse Core Ops, SparseCore 1:
  268.9 42.4 all-gather.10
  329.3 28.4 all-gather.8
  360.0 41.5 all-gather.12
  408.4 36.3 reduce-scatter.6
  451.1 28.4 all-gather.14
  533.3 28.3 all-gather.16
where the time goes:
time: 834 us; the launch traced here: 829 us
  waiting for transfers between devices  256 us (31%)
  matrix products  233 us (28%)
  blocking collectives  209 us (25%)
  other arithmetic  84.7 us (10%)
  local copies, waits for them, and re-layouts  28.9 us (3%)
  between operations  16 us (2%)
    reduce_scatter x1, waiting for transfers between devices, local(): lax.psum_scatter(attn_terms, 'tensor', scatter_dimension=0, tiled=True)  58.4 us
    dot_general x17, matrix products, matrix_product(): return jnp.dot(left, right, preferred_element_type=jnp.float32)  46.5 us
    dot_general x8, matrix products, block_scores(): jnp.einsum('qhe,khe->hqk', q_blk, key_heads, preferred_element_type=jnp.f...  44.1 us
    reduce_scatter x1, waiting for transfers between devices, local(): lax.psum_scatter(matrix_product(grad_hidden, full_in.T).astype(jnp.bfloat...  38.1 us
    psum x1, blocking collectives, local(): a_sums = lax.psum((grad_a_query, grad_a_value), ('dp', 'tensor'))  37.9 us
    psum x1, blocking collectives, local(): b_sums = lax.psum((query_up_gradient, value_up_gradient), 'dp')  37.7 us
    all_gather x1, waiting for transfers between devices, local(): lax.all_gather(w_down, 'dp', axis=1, tiled=True)  36.4 us
    reduce_scatter x1, waiting for transfers between devices, local(): lax.psum_scatter(matrix_product(acted, full_down).astype(jnp.bfloat16), '...  36.3 us
  transfers between devices with their start and end apart: 10, of which 7 were waited for; matrix products, arithmetic and copies ran while one was open for 2% of the time, Pallas kernels for 0%

commit v1 on v0

v1 whole, which is shorter than its diff:
```python
import functools

import jax
import jax.numpy as jnp
from jax import lax
from jax.experimental import pallas as pl
from jax.experimental.pallas import tpu as pltpu
from jax.sharding import PartitionSpec as P

HEAD_DIM = 64
PAIR = 2 * HEAD_DIM
Q_BLOCK = 256
K_BLOCK = 512
ADAPTER_SCALE = 2.0
SCORE_SCALE = HEAD_DIM ** (-0.5)
LOG2_SCALE = SCORE_SCALE * 1.4426950408889634
NEG_FILL = -1e30
LN_EPS = 1e-05
VMEM_LIMIT = 56 * 1024 * 1024


def dot_nn(left, right):
    return jnp.dot(left, right, preferred_element_type=jnp.float32)


def dot_nt(left, right):
    return lax.dot_general(
        left, right, (((1,), (1,)), ((), ())), preferred_element_type=jnp.float32
    )


def dot_tn(left, right):
    return lax.dot_general(
        left, right, (((0,), (0,)), ((), ())), preferred_element_type=jnp.float32
    )


def norm_forward(row_vals, gain_vals, offset):
    middle = jnp.mean(row_vals, axis=-1, keepdims=True)
    centred = row_vals - middle
    inverse = lax.rsqrt(jnp.mean(centred * centred, axis=-1, keepdims=True) + LN_EPS)
    normed = centred * inverse
    return (normed * gain_vals + offset, normed, inverse)


def norm_backward(grad_out, normed, inverse, gain_vals):
    grad_n = grad_out * gain_vals
    return inverse * (
        grad_n
        - jnp.mean(grad_n, axis=-1, keepdims=True)
        - normed * jnp.mean(grad_n * normed, axis=-1, keepdims=True)
    )


def gelu_parts(hidden):
    cdf_part = 0.5 * (1.0 + lax.erf(hidden * 0.7071067811865476))
    density = jnp.exp(-0.5 * hidden * hidden) * 0.3989422804014327
    return (hidden * cdf_part, cdf_part + hidden * density)


def block_span(lengths_ref, first_row, rows, total_rows):
    low = jnp.int32(0)
    high = jnp.int32(total_rows)
    end = jnp.int32(0)
    for slot in range(lengths_ref.shape[1]):
        end = end + lengths_ref[0, slot]
        low = jnp.where(end <= first_row, jnp.maximum(low, end), low)
        high = jnp.where(end > first_row + rows - 1, jnp.minimum(high, end), high)
    return low, high


def row_bounds(lengths_ref, first_row, rows, total_rows):
    place = first_row + lax.broadcasted_iota(jnp.int32, (1, rows), 1)
    begin = jnp.zeros((1, rows), jnp.int32)
    finish = jnp.full((1, rows), total_rows, jnp.int32)
    end = jnp.int32(0)
    for slot in range(lengths_ref.shape[1]):
        end = end + lengths_ref[0, slot]
        done = place >= end
        begin = jnp.where(done, jnp.maximum(begin, end), begin)
        finish = jnp.where(done, finish, jnp.minimum(finish, end))
    return begin, finish


def stack_pair(block):
    lane = lax.broadcasted_iota(jnp.int32, block.shape, 1)
    zero = jnp.zeros_like(block)
    return jnp.concatenate(
        [jnp.where(lane < HEAD_DIM, block, zero), jnp.where(lane >= HEAD_DIM, block, zero)],
        axis=0,
    )


def unstack_pair(block, rows):
    joined = jnp.concatenate([block[:HEAD_DIM, :rows], block[HEAD_DIM:, rows:]], axis=0)
    return joined.T


def window_mask(step, low, begin, finish, total_rows):
    wanted = low + step * K_BLOCK
    start = pl.multiple_of(jnp.minimum(wanted, total_rows - K_BLOCK), 128)
    key_at = start + lax.broadcasted_iota(jnp.int32, (K_BLOCK, begin.shape[1]), 0)
    return start, (key_at >= jnp.maximum(begin, wanted)) & (key_at < finish)


def forward_kernel(lengths_ref, q_ref, k_ref, v_ref, out_ref, lse_ref):
    rows = q_ref.shape[0]
    total_rows = k_ref.shape[0]
    base = lax.axis_index("tensor") * rows
    for q_at in range(rows // Q_BLOCK):
        first_row = base + q_at * Q_BLOCK
        low, high = block_span(lengths_ref, first_row, Q_BLOCK, total_rows)
        low = (low // 128) * 128
        steps = (high - low + K_BLOCK - 1) // K_BLOCK
        begin, finish = row_bounds(lengths_ref, first_row, Q_BLOCK, total_rows)
        q_rows = slice(q_at * Q_BLOCK, (q_at + 1) * Q_BLOCK)
        for pair in range(q_ref.shape[1] // PAIR):
            lanes = slice(pair * PAIR, (pair + 1) * PAIR)
            q_two = stack_pair(q_ref[q_rows, lanes])

            def body(step, carry, q_two=q_two, lanes=lanes, low=low, begin=begin, finish=finish):
                top, total, acc = carry
                start, allowed = window_mask(step, low, begin, finish, total_rows)
                keys = k_ref[pl.ds(start, K_BLOCK), lanes]
                values = v_ref[pl.ds(start, K_BLOCK), lanes]
                both = jnp.concatenate([allowed, allowed], axis=1)
                scores = jnp.where(both, dot_nt(keys, q_two), NEG_FILL)
                new_top = jnp.maximum(top, jnp.max(scores, axis=0, keepdims=True))
                probs = jnp.exp2((scores - new_top) * LOG2_SCALE)
                shrink = jnp.exp2((top - new_top) * LOG2_SCALE)
                total = total * shrink + jnp.sum(probs, axis=0, keepdims=True)
                acc = acc * shrink + dot_tn(values, probs.astype(jnp.bfloat16))
                return new_top, total, acc

            top, total, acc = lax.fori_loop(
                0,
                steps,
                body,
                (
                    jnp.full((1, 2 * Q_BLOCK), NEG_FILL, jnp.float32),
                    jnp.zeros((1, 2 * Q_BLOCK), jnp.float32),
                    jnp.zeros((PAIR, 2 * Q_BLOCK), jnp.float32),
                ),
            )
            out_ref[q_rows, lanes] = unstack_pair(acc / total, Q_BLOCK).astype(jnp.bfloat16)
            lse = top * LOG2_SCALE + jnp.log2(total)
            lse_ref[2 * pair : 2 * pair + 1, q_rows] = lse[:, :Q_BLOCK]
            lse_ref[2 * pair + 1 : 2 * pair + 2, q_rows] = lse[:, Q_BLOCK:]


def backward_kernel(
    lengths_ref,
    q_ref,
    k_ref,
    v_ref,
    ctx_ref,
    lse_ref,
    grad_ref,
    gq_ref,
    gk_ref,
    gv_ref,
    gk_acc,
    gv_acc,
):
    rows = q_ref.shape[0]
    total_rows = k_ref.shape[0]
    base = lax.axis_index("tensor") * rows
    gk_acc[...] = jnp.zeros_like(gk_acc)
    gv_acc[...] = jnp.zeros_like(gv_acc)
    for q_at in range(rows // Q_BLOCK):
        first_row = base + q_at * Q_BLOCK
        low, high = block_span(lengths_ref, first_row, Q_BLOCK, total_rows)
        low = (low // 128) * 128
        steps = (high - low + K_BLOCK - 1) // K_BLOCK
        begin, finish = row_bounds(lengths_ref, first_row, Q_BLOCK, total_rows)
        q_rows = slice(q_at * Q_BLOCK, (q_at + 1) * Q_BLOCK)
        for pair in range(q_ref.shape[1] // PAIR):
            lanes = slice(pair * PAIR, (pair + 1) * PAIR)
            q_two = stack_pair(q_ref[q_rows, lanes])
            grad_blk = grad_ref[q_rows, lanes]
            grad_two = stack_pair(grad_blk)
            product = (grad_blk.astype(jnp.float32) * ctx_ref[q_rows, lanes].astype(jnp.float32)).T
            row_dot = jnp.concatenate(
                [
                    jnp.sum(product[:HEAD_DIM], axis=0, keepdims=True),
                    jnp.sum(product[HEAD_DIM:], axis=0, keepdims=True),
                ],
                axis=1,
            )
            lse = jnp.concatenate(
                [
                    lse_ref[2 * pair : 2 * pair + 1, q_rows],
                    lse_ref[2 * pair + 1 : 2 * pair + 2, q_rows],
                ],
                axis=1,
            )

            def body(
                step,
                acc,
                q_two=q_two,
                grad_two=grad_two,
                row_dot=row_dot,
                lse=lse,
                lanes=lanes,
                low=low,
                begin=begin,
                finish=finish,
            ):
                start, allowed = window_mask(step, low, begin, finish, total_rows)
                window = pl.ds(start, K_BLOCK)
                keys = k_ref[window, lanes]
                values = v_ref[window, lanes]
                both = jnp.concatenate([allowed, allowed], axis=1)
                scores = jnp.where(both, dot_nt(keys, q_two), NEG_FILL)
                probs = jnp.exp2(scores * LOG2_SCALE - lse)
                grad_probs = dot_nt(values, grad_two)
                grad_scores = (probs * (grad_probs - row_dot)).astype(jnp.bfloat16)
                gk_acc[window, lanes] += dot_nn(grad_scores, q_two)
                gv_acc[window, lanes] += dot_nn(probs.astype(jnp.bfloat16), grad_two)
                return acc + dot_tn(keys, grad_scores)

            acc = lax.fori_loop(0, steps, body, jnp.zeros((PAIR, 2 * Q_BLOCK), jnp.float32))
            gq_ref[q_rows, lanes] = (unstack_pair(acc, Q_BLOCK) * SCORE_SCALE).astype(jnp.bfloat16)
    gk_ref[...] = (gk_acc[...] * SCORE_SCALE).astype(jnp.bfloat16)
    gv_ref[...] = gv_acc[...].astype(jnp.bfloat16)


VMEM_SPEC = pl.BlockSpec(memory_space=pltpu.VMEM)
SMEM_SPEC = pl.BlockSpec(memory_space=pltpu.SMEM)


def attend_forward(lengths, q_own, k_all, v_all):
    rows, width = q_own.shape
    heads = width // HEAD_DIM
    return pl.pallas_call(
        forward_kernel,
        out_shape=(
            jax.ShapeDtypeStruct((rows, width), jnp.bfloat16),
            jax.ShapeDtypeStruct((-(-heads // 8) * 8, rows), jnp.float32),
        ),
        in_specs=[SMEM_SPEC] + [VMEM_SPEC] * 3,
        out_specs=(VMEM_SPEC, VMEM_SPEC),
        compiler_params=pltpu.CompilerParams(vmem_limit_bytes=VMEM_LIMIT),
        name="attend_forward",
    )(lengths, q_own, k_all, v_all)


def attend_backward(lengths, q_own, k_all, v_all, context, lse, grad_context):
    rows, width = q_own.shape
    total_rows = k_all.shape[0]
    return pl.pallas_call(
        backward_kernel,
        out_shape=(
            jax.ShapeDtypeStruct((rows, width), jnp.bfloat16),
            jax.ShapeDtypeStruct((total_rows, width), jnp.bfloat16),
            jax.ShapeDtypeStruct((total_rows, width), jnp.bfloat16),
        ),
        in_specs=[SMEM_SPEC] + [VMEM_SPEC] * 6,
        out_specs=(VMEM_SPEC,) * 3,
        scratch_shapes=[
            pltpu.VMEM((total_rows, width), jnp.float32),
            pltpu.VMEM((total_rows, width), jnp.float32),
        ],
        compiler_params=pltpu.CompilerParams(vmem_limit_bytes=VMEM_LIMIT),
        name="attend_backward",
    )(lengths, q_own, k_all, v_all, context, lse, grad_context)


def local(
    tokens,
    query_weight,
    w_key,
    value_weight,
    w_out,
    w_in,
    w_down,
    gain_attn,
    shift_attn,
    gain_ffn,
    shift_ffn,
    query_down_factor,
    query_up_factor,
    value_down_factor,
    value_up_factor,
    lengths,
    cotangent,
):
    slim = query_weight.shape[1]
    attn_pack = jnp.concatenate([query_weight, w_key, value_weight, w_out.T], axis=1)
    packed = jnp.stack([attn_pack, w_in, w_down.T])
    packed = lax.all_gather(packed, "dp", axis=1, tiled=True)
    packed = lax.all_gather(packed, "tensor", axis=0)
    width = packed.shape[2]
    attn_full = packed[:, 0].reshape(-1, width, 4, slim).transpose(2, 1, 0, 3)
    attn_full = attn_full.reshape(4, width, width)
    w_q, w_k, w_v, w_o_t = (attn_full[i] for i in range(4))
    full_in = packed[:, 1].transpose(1, 0, 2).reshape(width, -1)
    full_down_t = packed[:, 2].transpose(1, 0, 2).reshape(width, -1)
    query_up = lax.all_gather(query_up_factor, "tensor", axis=1, tiled=True)
    value_up = lax.all_gather(value_up_factor, "tensor", axis=1, tiled=True)
    rows_all = lax.all_gather(tokens, "tensor", axis=0, tiled=True)

    u_query = dot_nn(tokens, query_down_factor).astype(jnp.bfloat16)
    q_own = (dot_nn(tokens, w_q) + ADAPTER_SCALE * dot_nn(u_query, query_up)).astype(jnp.bfloat16)
    k_all = dot_nn(rows_all, w_k).astype(jnp.bfloat16)
    u_value = dot_nn(rows_all, value_down_factor).astype(jnp.bfloat16)
    v_all = (dot_nn(rows_all, w_v) + ADAPTER_SCALE * dot_nn(u_value, value_up)).astype(jnp.bfloat16)

    context, lse = attend_forward(lengths, q_own, k_all, v_all)

    first_f, normed_one, inverse_one = norm_forward(
        tokens.astype(jnp.float32) + dot_nt(context, w_o_t), gain_attn, shift_attn
    )
    first = first_f.astype(jnp.bfloat16)
    hidden = dot_nn(first, full_in)
    acted_f, slope = gelu_parts(hidden)
    ffn_out = dot_nt(acted_f.astype(jnp.bfloat16), full_down_t)
    mixed_f, normed_two, inverse_two = norm_forward(
        first.astype(jnp.float32) + ffn_out, gain_ffn, shift_ffn
    )
    mixed = mixed_f.astype(jnp.bfloat16)
    grad_two = norm_backward(cotangent.astype(jnp.float32), normed_two, inverse_two, gain_ffn)
    grad_hidden = (dot_nn(grad_two.astype(jnp.bfloat16), full_down_t) * slope).astype(jnp.bfloat16)
    grad_first = grad_two + dot_nt(grad_hidden, full_in)
    grad_one = norm_backward(grad_first, normed_one, inverse_one, gain_attn)
    grad_context = dot_nn(grad_one.astype(jnp.bfloat16), w_o_t).astype(jnp.bfloat16)

    grad_q, grad_k, grad_v = attend_backward(
        lengths, q_own, k_all, v_all, context, lse, grad_context
    )
    rows = tokens.shape[0]
    grad_uq = ADAPTER_SCALE * dot_nt(grad_q, query_up)
    grad_uv = ADAPTER_SCALE * dot_nt(grad_v, value_up)
    grad_bq = ADAPTER_SCALE * dot_tn(u_query, grad_q)
    grad_bv = ADAPTER_SCALE * dot_tn(u_value, grad_v)
    grad_aq = dot_tn(tokens, grad_uq.astype(jnp.bfloat16))
    grad_av = dot_tn(rows_all, grad_uv.astype(jnp.bfloat16))
    grad_rows = (
        dot_nt(grad_k, w_k)
        + dot_nt(grad_v, w_v)
        + dot_nt(grad_uv.astype(jnp.bfloat16), value_down_factor)
    )
    own_rows = dot_nt(grad_q, w_q) + dot_nt(grad_uq.astype(jnp.bfloat16), query_down_factor)
    shared = lax.psum_scatter(
        grad_rows.astype(jnp.bfloat16), "tensor", scatter_dimension=0, tiled=True
    )
    grad_tokens = (grad_one + own_rows + shared.astype(jnp.float32)).astype(jnp.bfloat16)
    grad_aq, grad_av, grad_bq, grad_bv = lax.psum(
        (grad_aq, grad_av, grad_bq, grad_bv), ("dp", "tensor")
    )
    at = lax.axis_index("tensor") * slim
    grad_bq = lax.dynamic_slice_in_dim(grad_bq, at, slim, 1)
    grad_bv = lax.dynamic_slice_in_dim(grad_bv, at, slim, 1)
    return (mixed, grad_tokens, grad_aq, grad_bq, grad_av, grad_bv)


def solution(mesh):
    return jax.shard_map(
        local,
        mesh=mesh,
        in_specs=(
            P(("dp", "tensor"), None),
            P("dp", "tensor"),
            P("dp", "tensor"),
            P("dp", "tensor"),
            P("tensor", "dp"),
            P("dp", "tensor"),
            P("tensor", "dp"),
            P(),
            P(),
            P(),
            P(),
            P(),
            P(None, "tensor"),
            P(),
            P(None, "tensor"),
            P("dp", None),
            P(("dp", "tensor"), None),
        ),
        out_specs=(
            P(("dp", "tensor"), None),
            P(("dp", "tensor"), None),
            P(),
            P(None, "tensor"),
            P(),
            P(None, "tensor"),
        ),
        check_vma=False,
    )
```

time: 834 us -> 518 us (0.62)
  blocking collectives: 209 us -> 10.4 us
  matrix products: 233 us -> 73.7 us
  other arithmetic: 84.7 us -> 4.93 us
  waiting for transfers between devices: 256 us -> 325 us
  Pallas kernels: 0 us -> 34.7 us
  local copies, waits for them, and re-layouts: 28.9 us -> 45.7 us
    dot_general x51 -> x23, matrix products: 233 us -> 73.7 us  [the longest x10 45.4 us: dot_nt(): lax.dot_general(left, right, (((1,), (1,)), ((), ())), preferred_element_...]
    reduce_scatter x3 -> x0, waiting for transfers between devices: 133 us -> none  [the longest x1 58.4 us: local(): lax.psum_scatter(attn_terms, 'tensor', scatter_dimension=0, tiled=True)]
    all_gather x4 -> x2, blocking collectives: 133 us -> 10.4 us  [the longest x1 5.18 us: local(): value_up = lax.all_gather(value_up_factor, 'tensor', axis=1, tiled=True)]
    psum x0 -> x1, waiting for transfers between devices: none -> 112 us  [local(): lax.psum((grad_aq, grad_av, grad_bq, grad_bv), ('dp', 'tensor'))]
    psum x2 -> x0, blocking collectives: 75.6 us -> none  [the longest x1 37.9 us: local(): a_sums = lax.psum((grad_a_query, grad_a_value), ('dp', 'tensor'))]
    all_gather x6 -> x3, waiting for transfers between devices: 121 us -> 174 us  [the longest x1 89.8 us: local(): packed = lax.all_gather(packed, 'tensor', axis=0)]
    reduce_scatter x1, waiting for transfers between devices: 0.01 us -> 38.5 us  [local(): lax.psum_scatter(grad_rows.astype(jnp.bfloat16), 'tensor', scatter_dimens...]
    pallas_call x0 -> x2, Pallas kernels: none -> 34.7 us  [the longest x1 20.3 us: attend_backward(): pl.pallas_call(backward_kernel, out_shape=(jax.ShapeDtypeStruct((rows, wi...]
  transfers between devices with their start and end apart: 10 -> 5, of which waited for: 7 -> 5; matrix products, arithmetic and copies ran while one was open for 2% -> 3% of each run, Pallas kernels for 0% -> 0%
where the time goes in v1:
time: 518 us; the launch traced here: 509 us
  waiting for transfers between devices  325 us (63%)
  matrix products  73.7 us (14%)
  local copies, waits for them, and re-layouts  45.7 us (9%)
  Pallas kernels  34.7 us (7%)
  between operations  14.3 us (3%)
  blocking collectives  10.4 us (2%)
    psum x1, waiting for transfers between devices, local(): lax.psum((grad_aq, grad_av, grad_bq, grad_bv), ('dp', 'tensor'))  112 us
    all_gather x1, waiting for transfers between devices, local(): packed = lax.all_gather(packed, 'tensor', axis=0)  89.8 us
    all_gather x1, waiting for transfers between devices, local(): packed = lax.all_gather(packed, 'dp', axis=1, tiled=True)  67.2 us
    dot_general x10, matrix products, dot_nt(): lax.dot_general(left, right, (((1,), (1,)), ((), ())), preferred_element_...  45.4 us
    reduce_scatter x1, waiting for transfers between devices, local(): lax.psum_scatter(grad_rows.astype(jnp.bfloat16), 'tensor', scatter_dimens...  38.5 us
    dot_general x9, matrix products, dot_nn(): return jnp.dot(left, right, preferred_element_type=jnp.float32)  24.4 us
    pallas_call x1, Pallas kernels, attend_backward(): pl.pallas_call(backward_kernel, out_shape=(jax.ShapeDtypeStruct((rows, wi...  20.3 us
    slice x2, local copies, waits for them, and re-layouts, local(): attn_full = packed[:, 0].reshape(-1, width, 4, slim).transpose(2, 1, 0, 3)  17.6 us
  transfers between devices with their start and end apart: 5, of which 5 were waited for; matrix products, arithmetic and copies ran while one was open for 3% of the time, Pallas kernels for 0%

profile of v1, /device:TPU:0, one launch (start us, length us, event | category | flops | bytes accessed | tf_op | source)
XLA Modules:
  0.0 508.7 jit_solution(15945183199476226742)
XLA Ops:
  7.2 0.9 copy.42
  8.1 1.0 maximum_bitcast_fusion
  9.1 1.8 pad_maximum_fusion
  10.9 0.7 all-gather.9.cloned.1.call-update
  11.7 67.2 %all-gather.7.cloned.1.call-done = bf16[3,768,768]{2,1,0:T(8,128)(2,1)} async-done(((bf16[3,96,768]{2,1,0:T(8,128)(2,1)}), bf16[3,768,768]{2,1,0:T(8,128)(2,1)}) %all-gather.7.cloned.1.call-update) | async-done | bytes 3538960 | tf_op jit(solution)/shard_map/all_gather | solution.py:292
  79.0 0.6 copy-done.28
  79.6 5.2 %all-gather.1 = bf16[4,192,8]{1,2,0:T(8,128)(2,1)S(1)} all-gather(bf16[1,192,8]{1,2,0:T(8,128)(2,1)S(1)} %bitcast.111), channel_id=1, replica_groups=mesh['dp'=8,'tensor'=4] {'tensor'}, dimensions={0}, use_global_device_ids=true | all-gather | bytes 15360 | tf_op jit(solution)/shard_map/all_gather | solution.py:300
  84.9 5.2 %all-gather.2 = bf16[4,192,8]{1,2,0:T(8,128)(2,1)S(1)} all-gather(bf16[1,192,8]{1,2,0:T(8,128)(2,1)S(1)} %bitcast.112), channel_id=1, replica_groups=mesh['dp'=8,'tensor'=4] {'tensor'}, dimensions={0}, use_global_device_ids=true | all-gather | bytes 15360 | tf_op jit(solution)/shard_map/all_gather | solution.py:301
  90.5 17.1 %all-gather.9.cloned.1.call-done = bf16[2048,768]{1,0:T(8,128)(2,1)} async-done(((bf16[512,768]{1,0:T(8,128)(2,1)}), bf16[2048,768]{1,0:T(8,128)(2,1)}) %all-gather.9.cloned.1.call-update) | async-done | bytes 3145744 | tf_op jit(solution)/shard_map/all_gather | solution.py:302
  107.6 2.8 convolution_convert_fusion.1
  110.4 89.8 %all-gather.11.cloned.1.call-done = bf16[12,768,768]{2,1,0:T(8,128)(2,1)} async-done(((bf16[3,768,768]{2,1,0:T(8,128)(2,1)}), bf16[12,768,768]{2,1,0:T(8,128)(2,1)}) %all-gather.11.cloned.1.call-update) | async-done | bytes 14155792 | tf_op jit(solution)/shard_map/all_gather | solution.py:293
  200.2 11.0 %fusion.30 = (bf16[4,1,768,768]{3,2,1,0:T(8,128)(2,1)}, bf16[768,4,768]{2,0,1:T(8,128)(2,1)}, bf16[768,4,768]{2,0,1:T(8,128)(2,1)}) fusion(bf16[4,3,768,768]{3,2,1,0:T(8,128)(2,1)} %bitcast.93), kind=kLoop, calls=%fused_computation.69 | loop fusion | bytes 28311552 | tf_op jit(solution)/shard_map/slice | solution.py:295
  211.2 6.7 %copy.50 = bf16[768,4,768]{0,2,1:T(8,128)(2,1)} copy(bf16[768,4,768]{2,0,1:T(8,128)(2,1)} %get-tuple-element.25) | data formatting | bytes 9437184 | tf_op jit(solution)/shard_map/transpose | solution.py:299
  217.8 6.6 %copy.49 = bf16[768,4,768]{0,2,1:T(8,128)(2,1)} copy(bf16[768,4,768]{2,0,1:T(8,128)(2,1)} %get-tuple-element.26) | data formatting | bytes 9437184 | tf_op jit(solution)/shard_map/transpose | solution.py:298
  224.5 6.7 %copy.43 = bf16[4,1,768,768]{2,3,0,1:T(8,128)(2,1)} copy(bf16[4,1,768,768]{3,2,1,0:T(8,128)(2,1)} %get-tuple-element.24) | data formatting | bytes 9437184 | tf_op jit(solution)/shard_map/slice | solution.py:295
  231.2 3.8 fusion.31
  235.0 0.8 fusion.36
  236.0 1.3 fusion.10.q_ref
  237.3 1.1 copy-done.1
  238.4 2.7 fusion.37
  241.2 2.7 fusion.6.v_ref
  243.9 4.0 fusion.8.k_ref
  248.0 14.3 %attend_forward.1 = (bf16[512,768]{1,0:T(8,128)(2,1)}, f32[16,512]{1,0:T(8,128)}) custom-call(s32[1,32]{1,0:T(1,128)} %lengths_ref.3, bf16[512,768]{1,0:T(8,128)(2,1)} %fusion.10.q_ref, bf16[2048,768]{1,0:T(8,128)(2,1)} %fusion.8.k_ref, bf16[2048,768]{1,0:T(8,128)(2,1)} %fusion.6.v_ref), custom_call_target="tpu_custom_call" | custom-call | tf_op jit(solution)/shard_map/attend_forward/pallas_call | solution.py:236
  262.3 2.0 fusion.32
  265.1 5.6 %fusion.28 = f32[512,3072]{1,0:T(8,128)S(1)} fusion(bf16[768,3072]{0,1:T(8,128)(2,1)} %bitcast.98, f32[512,768]{1,0:T(8,128)S(1)} %get-tuple-element.33, f32[768]{0:T(1024)S(1)} %copy-done.31, f32[768]{0:T(1024)S(1)} %copy-done.32, f32[512]{0:T(512)S(1)} %add_rsqrt_fusion.1, f32[512]{0:T(512)S(1)} %broadcast_multiply_fusion.5), kind=kOutput, calls=%fused_computation.67 | convolution fusion | flops 2417885184 | bytes 12593152 | tf_op jit(solution)/shard_map/dot_general | solution.py:23
  270.7 3.2 fusion.33
  274.2 1.3 copy-done.18
  275.6 1.5 fusion.11
  277.1 14.3 %fusion.29 = (f32[512]{0:T(512)S(1)}, f32[512]{0:T(512)S(1)}, f32[512,768]{1,0:T(8,128)}) fusion(f32[512]{0:T(512)S(1)} %add_rsqrt_fusion.1, f32[512,768]{1,0:T(8,128)} %copy-done.7, f32[512]{0:T(512)S(1)} %broadcast_multiply_fusion.5, f32[768]{0:T(1024)S(1)} %copy-done.32, bf16[768,3072]{0,1:T(8,128)(2,1)} %bitcast.99, f32[512,3072]{1,0:T(8,128)} %copy-done.33, ...), kind=kOutput, calls=%fused_computation.68 | convolution fusion | flops 4857003008 | bytes 21256192 | tf_op jit(solution)/shard_map/dot_general | solution.py:27
  291.4 4.1 convolution_convert_fusion.2.grad_ref
  295.5 20.3 %attend_backward.1 = (bf16[512,768]{1,0:T(8,128)(2,1)}, bf16[2048,768]{1,0:T(8,128)(2,1)}, bf16[2048,768]{1,0:T(8,128)(2,1)}) custom-call(s32[1,32]{1,0:T(1,128)} %lengths_ref.3, bf16[512,768]{1,0:T(8,128)(2,1)} %fusion.10.q_ref, bf16[2048,768]{1,0:T(8,128)(2,1)} %fusion.8.k_ref, bf16[2048,768]{1,0:T(8,128)(2,1)} %fusion.6.v_ref, ...), custom_call_target="tpu_custom_call" | custom-call | tf_op jit(solution)/shard_map/attend_backward/pallas_call | solution.py:252
  315.9 7.3 %fusion.40 = f32[2048,768]{1,0:T(8,128)} fusion(bf16[2048,768]{1,0:T(8,128)(2,1)} %get-tuple-element.15, bf16[768,768]{0,1:T(8,128)(2,1)S(1)} %bitcast.105), kind=kOutput, calls=%fused_computation.77 | convolution fusion | flops 2415919104 | bytes 10616832 | tf_op jit(solution)/shard_map/dot_general | solution.py:27
  323.2 0.9 fusion.9
  324.6 0.8 convolution_multiply_fusion.2
  325.4 1.1 convolution_multiply_fusion.1
  326.9 4.5 fusion.39
  331.4 0.8 convolution_bitcast_fusion.1
  332.2 1.1 convolution_bitcast_fusion
  333.4 7.3 %add_convert_fusion = bf16[2048,768]{1,0:T(8,128)(2,1)} fusion(f32[2048,768]{1,0:T(8,128)} %fusion.39, f32[2048,768]{1,0:T(8,128)} %fusion.40, bf16[2048,8]{0,1:T(8,128)(2,1)S(1)} %fusion.9, bf16[768,8]{0,1:T(8,128)(2,1)S(1)} %copy-done), kind=kOutput, calls=%fused_computation.9 | convolution fusion | flops 29884416 | bytes 15773696 | tf_op jit(solution)/shard_map/dot_general | solution.py:27
  340.7 1.1 copy-done.10
  342.2 1.9 fusion.38
  344.1 111.5 %all-reduce.3.cloned.1.call-done = (f32[768,8]{0,1:T(8,128)}, f32[8,768]{1,0:T(8,128)}, f32[768,8]{0,1:T(8,128)}, f32[8,768]{1,0:T(8,128)}) async-done(((f32[768,8]{0,1:T(8,128)}, f32[8,768]{1,0:T(8,128)}, f32[768,8]{0,1:T(8,128)}, f32[8,768]{1,0:T(8,128)}), (f32[768,8]{0,1:T(8,128)}, f32[8,768]{1,0:T(8,128)}, f32[768,8]{0,1:T(8,128)}, f32[8,768]{1,0:T(8,128)})) %all-reduce.3.cloned.1.call-update) | async-done | bytes 98320 | tf_op jit(solution)/shard_map/psum | solution.py:349
  455.6 1.4 constant_dynamic-slice_fusion.1
  457.0 1.4 constant_dynamic-slice_fusion
  458.4 38.5 %reduce-scatter.2.cloned.1.call-done = bf16[512,768]{1,0:T(8,128)(2,1)} async-done(((bf16[2048,768]{1,0:T(8,128)(2,1)}), bf16[512,768]{1,0:T(8,128)(2,1)}) %reduce-scatter.2.cloned.1.call-update) | async-done | bytes 786448 | tf_op jit(solution)/shard_map/reduce_scatter | solution.py:345
  496.9 3.8 add_convert_fusion.1
  500.7 0.6 copy.58
  501.3 0.6 copy.59
  (93 shorter events, 3.3 us)
Async XLA Ops:
  7.2 100.4 %copy-start = (bf16[768,8]{0,1:T(8,128)(2,1)S(1)}, bf16[768,8]{0,1:T(8,128)(2,1)}, u32[]{:S(2)}) copy-start(bf16[768,8]{0,1:T(8,128)(2,1)} %param.30) | copy-start | bytes 36868
  7.2 71.8 %all-gather.7.cloned.1.call-start = ((), (), s32[]{:S(2)}) async-start(), calls=%async_computation.1 | async-start | bytes 3981312 | tf_op jit(solution)/shard_map/all_gather | solution.py:292
  10.9 96.7 %all-gather.9.cloned.1.call-start = ((), (), s32[]{:S(2)}) async-start(), calls=%async_computation.2 | async-start | bytes 3932160 | tf_op jit(solution)/shard_map/all_gather | solution.py:302
  11.7 188.5 %all-gather.11.cloned.1.call-start = ((), (), s32[]{:S(2)}) async-start(), calls=%async_computation.4 | async-start | bytes 17694720 | tf_op jit(solution)/shard_map/all_gather | solution.py:293
  78.9 0.7 copy-start.28
  78.9 6.0 %copy-start.29 = (bf16[8,192]{1,0:T(8,128)(2,1)S(1)}, bf16[8,192]{1,0:T(8,128)(2,1)}, u32[]{:S(2)}) copy-start(bf16[8,192]{1,0:T(8,128)(2,1)} %param.31) | copy-start | bytes 9220
  79.0 11.2 %copy-start.3 = (bf16[512,768]{1,0:T(8,128)(2,1)S(1)}, bf16[512,768]{1,0:T(8,128)(2,1)}, u32[]{:S(2)}) copy-start(bf16[512,768]{1,0:T(8,128)(2,1)} %param.17) | copy-start | bytes 2359300
  79.0 11.2 %copy-start.20 = (bf16[768,8]{0,1:T(8,128)(2,1)S(1)}, bf16[768,8]{0,1:T(8,128)(2,1)}, u32[]{:S(2)}) copy-start(bf16[768,8]{0,1:T(8,128)(2,1)} %param.28) | copy-start | bytes 36868
  79.0 376.6 %all-reduce.3.cloned.1.call-start = ((), (), s32[]{:S(2)}) async-start(), calls=%async_computation.5 | async-start | bytes 196608 | tf_op jit(solution)/shard_map/psum | solution.py:349
  231.1 3.8 copy-start.4
  235.0 1.0 copy-start.11
  235.0 2.3 copy-start.15
  235.0 8.9 %copy-start.13 = (bf16[1,768,4,192]{1,3,0,2:T(8,128)(2,1)}, bf16[1,768,4,192]{1,3,0,2:T(8,128)(2,1)S(1)}, u32[]{:S(2)}) copy-start(bf16[1,768,4,192]{1,3,0,2:T(8,128)(2,1)S(1)} %get-tuple-element.29) | copy-start | bytes 3538948
  235.0 3.5 copy-start.1
  248.0 14.3 %copy-start.17 = (bf16[1,768,4,192]{1,3,0,2:T(8,128)(2,1)S(1)}, bf16[1,768,4,192]{1,3,0,2:T(8,128)(2,1)}, u32[]{:S(2)}) copy-start(bf16[1,768,4,192]{1,3,0,2:T(8,128)(2,1)} %get-tuple-element.27) | copy-start | bytes 3538948
  264.3 6.3 %copy-start.7 = (f32[512,768]{1,0:T(8,128)}, f32[512,768]{1,0:T(8,128)S(1)}, u32[]{:S(2)}) copy-start(f32[512,768]{1,0:T(8,128)S(1)} %get-tuple-element.33) | copy-start | bytes 4718596
  264.3 0.7 copy-start.31
  264.3 0.7 copy-start.32
  264.3 6.3 %slice-start = ((s8[4718592]{0:T(1024)(128)(4,1)}), s8[4194304]{0:T(1024)(128)(4,1)S(1)}, s32[]{:S(2)}) async-start(s8[4718592]{0:T(1024)(128)(4,1)} %bitcast.95), calls=%async_computation.6 | async-start | bytes 8388608
  264.7 26.7 %copy-start.23 = (f32[512]{0:T(512)}, f32[512]{0:T(512)S(1)}, u32[]{:S(2)}) copy-start(f32[512]{0:T(512)S(1)} %add_rsqrt_fusion.1) | copy-start | bytes 6148
  265.1 5.6 %slice-start.1 = ((s8[4718592]{0:T(1024)(128)(4,1)}), s8[524288]{0:T(1024)(128)(4,1)S(1)}, s32[]{:S(2)}) async-start(s8[4718592]{0:T(1024)(128)(4,1)} %bitcast.95), calls=%async_computation.7 | async-start | bytes 1048576
  270.6 3.2 copy-start.33
  273.9 3.3 copy-start.6
  273.9 1.7 copy-start.18
  273.9 1.7 copy-start.26
  273.9 1.7 copy-start.27
  291.4 4.1 copy-start.24
  291.4 4.1 copy-start.25
  295.5 20.3 %copy-start.16 = (bf16[1,768,4,192]{1,3,0,2:T(8,128)(2,1)S(1)}, bf16[1,768,4,192]{1,3,0,2:T(8,128)(2,1)}, u32[]{:S(2)}) copy-start(bf16[1,768,4,192]{1,3,0,2:T(8,128)(2,1)} %copy-done.15) | copy-start | bytes 3538948
  315.9 7.3 %copy-start.2 = (bf16[2048,768]{1,0:T(8,128)(2,1)S(1)}, bf16[2048,768]{1,0:T(8,128)(2,1)}, u32[]{:S(2)}) copy-start(bf16[2048,768]{1,0:T(8,128)(2,1)} %get-tuple-element.15) | copy-start | bytes 9437188
  323.2 1.1 copy-start.9
  324.3 2.3 copy-start.30
  324.6 6.8 %copy-start.19 = (bf16[512,8]{0,1:T(8,128)(2,1)}, bf16[512,8]{0,1:T(8,128)(2,1)S(1)}, u32[]{:S(2)}) copy-start(bf16[512,8]{0,1:T(8,128)(2,1)S(1)} %fusion.12) | copy-start | bytes 24580
  325.4 1.5 copy-start.14
  326.9 4.5 copy-start.5
  333.3 163.5 %reduce-scatter.2.cloned.1.call-start = ((), (), s32[]{:S(2)}) async-start(), calls=%async_computation.3 | async-start | bytes 3932160 | tf_op jit(solution)/shard_map/reduce_scatter | solution.py:345
  340.7 1.1 copy-start.10
  340.7 1.5 copy-start.12
  342.2 154.7 %copy-start.8 = (f32[512,768]{1,0:T(8,128)S(1)}, f32[512,768]{1,0:T(8,128)}, u32[]{:S(2)}) copy-start(f32[512,768]{1,0:T(8,128)} %copy-done.7) | copy-start | bytes 4718596
  458.4 42.3 %copy-start.22 = (f32[768,8]{0,1:T(8,128)S(1)}, f32[768,8]{0,1:T(8,128)}, u32[]{:S(2)}) copy-start(f32[768,8]{0,1:T(8,128)} %get-tuple-element.41) | copy-start | bytes 73732
  458.4 42.9 %copy-start.21 = (f32[768,8]{0,1:T(8,128)S(1)}, f32[768,8]{0,1:T(8,128)}, u32[]{:S(2)}) copy-start(f32[768,8]{0,1:T(8,128)} %get-tuple-element.43) | copy-start | bytes 73732
Sparse Core Ops, SparseCore 0:
  11.0 67.8 all-gather.6
  80.5 27.0 all-gather.8
  109.2 90.9 all-gather.10
  333.5 122.1 all-reduce.2
  458.0 38.8 reduce-scatter.1
